TPU v7x, 128 devices: a whole 4x4x4 slice. The times are simulated.
128 devices in a mesh: depth: 16 (over y, x), rows: 8 (over z, core).
Axes of the slice: x: 4, y: 4, z: 4, core: 2. Of those that a mesh axis runs over, the one named last changes fastest.
Arguments:
- coarse: bfloat16 [272, 128, 1024], P('depth', 'rows'), may hold values from -6 to 6
- detail: bfloat16 [512, 256, 2048], P('depth', 'rows'), may hold values from -3.59375 to 3.59375
- layout: int32 [2048], replicated, may hold values from 0 to 2047, each once
- view_order: int32 [16], replicated, may hold values from 0 to 15, as said below
Outputs:
- frame: float32 [4, 256, 2048], P(None, 'rows', 'depth')
Inputs may be any that keep to these rules, and one draw needn't show every extreme that they name: layout is a permutation of the columns. view_order[b] is b xor one number below 16, the same for all bricks, so every aligned block of 2, 4, 8 ... bricks holds an aligned block of ranks.
All inputs are finite; a program needn't handle non-finite values.
Results may differ from a plain program's by a relative error of at most 0.0003.
Values may be sent and summed in bfloat16 or wider, within the bound.
No kernel may reach another device: no remote copies, remote signals or barrier semaphores. Data moves between devices by JAX's collectives and lax.ppermute only.
A program may use at most 192 MiB of HBM per device.

v0:
```python
import jax
import jax.numpy as jnp
from jax import lax
from jax.sharding import PartitionSpec as P


def shifted(value, axis, by):
    peers = lax.axis_size(axis)
    return lax.ppermute(value, axis, [(i, (i + by) % peers) for i in range(peers)])


def padded_2(cells, sides, width):
    for axis, dim in sides:
        count = lax.axis_size(axis)
        head = lax.slice_in_dim(cells, 0, width, axis=dim)
        tail = lax.slice_in_dim(cells, cells.shape[dim] - width, cells.shape[dim], axis=dim)
        cells = jnp.concatenate(
            [
                lax.ppermute(tail, axis, [(i, (i + 1) % count) for i in range(count)]),
                cells,
                lax.ppermute(head, axis, [((i + 1) % count, i) for i in range(count)]),
            ],
            axis=dim,
        )
    return cells


def widen_cols(coarse_vals):
    next_cols = jnp.roll(coarse_vals, -1, axis=-1)
    midway = 0.5 * (coarse_vals + next_cols)
    return jnp.stack([coarse_vals, midway], axis=-1).reshape(
        coarse_vals.shape[:-1] + (2 * coarse_vals.shape[-1],)
    )


def lengthen(coarse_vals, next_rows):
    midway = 0.5 * (coarse_vals + next_rows)
    return jnp.stack([coarse_vals, midway], axis=2).reshape(
        (coarse_vals.shape[0], 2 * coarse_vals.shape[1], coarse_vals.shape[2])
    )


def deepen(coarse_vals):
    midway = 0.5 * (coarse_vals[:-1] + coarse_vals[1:])
    return jnp.stack([coarse_vals[:-1], midway], axis=1).reshape(
        (2 * (coarse_vals.shape[0] - 1),) + coarse_vals.shape[1:]
    )


def shade_brick(values, row_above, row_below, total_depth):
    grad_x = 0.5 * (jnp.roll(values, -1, axis=2) - jnp.roll(values, 1, axis=2))
    grad_y = 0.5 * (row_below - row_above)
    upper_plane = jnp.concatenate([values[1:], values[-1:]], 0)
    lower_plane = jnp.concatenate([values[:1], values[:-1]], 0)
    grad_z = 0.5 * (upper_plane - lower_plane)
    facing = jnp.abs(0.48 * grad_x + 0.6 * grad_y + 0.64 * grad_z)
    shading = 0.35 + 0.65 * facing / jnp.sqrt(
        1.0 + grad_x * grad_x + grad_y * grad_y + grad_z * grad_z
    )
    optical = 2.0 / total_depth * jax.nn.softplus(1.5 * values - 0.5)
    before = jnp.cumsum(optical, axis=0) - optical
    weight = jnp.exp(-before) * -jnp.expm1(-optical) * shading
    shaded = jnp.stack(
        [
            jnp.sum(weight * jax.nn.sigmoid(2.0 * values), 0),
            jnp.sum(weight * jax.nn.sigmoid(-values), 0),
            jnp.sum(weight * jnp.exp(-0.5 * values * values), 0),
        ],
        0,
    )
    through = jnp.exp(-jnp.sum(optical, 0))
    return (shaded, through)


def on_device(coarse, detail, layout, view_order):
    depth_count = lax.axis_size("depth")
    planes = detail.shape[0]
    total_depth = planes * depth_count
    widened = widen_cols(coarse.astype(jnp.float32))
    following = shifted(coarse[:, :1, :], "rows", -1)
    widened_next = widen_cols(following.astype(jnp.float32))
    lengthened = lengthen(widened, jnp.concatenate([widened[:, 1:], widened_next], 1))
    values_here = deepen(lengthened) + jnp.take(detail, layout, axis=2).astype(jnp.float32)
    padded = padded_2(values_here, (("rows", 1),), 1)
    values = padded[:, 1:-1]
    shaded, through = shade_brick(values, padded[:, :-2], padded[:, 2:], total_depth)
    my_index = lax.axis_index("depth")
    my_rank = lax.dynamic_index_in_dim(view_order, my_index, keepdims=False)
    all_ones = jnp.ones_like(through)
    pieces_here = lax.all_gather(through[None], "depth", axis=0, tiled=True)
    nearer = all_ones
    overall = all_ones
    in_front = jnp.where((view_order < my_rank)[:, None, None], pieces_here, 1.0)
    nearer, overall = (nearer * jnp.prod(in_front, 0), overall * jnp.prod(pieces_here, 0))
    summed = lax.psum_scatter(nearer[None] * shaded, "depth", scatter_dimension=2, tiled=True)
    block_cols = summed.shape[2]
    own_through = lax.dynamic_slice_in_dim(overall, my_index * block_cols, block_cols, 1)
    return jnp.concatenate([summed, (1.0 - own_through)[None]], 0)


def solution(mesh):
    in_specs = (P("depth", "rows", None), P("depth", "rows", None), P(), P())
    out_specs = P(None, "rows", "depth")
    return jax.shard_map(
        on_device, mesh=mesh, in_specs=in_specs, out_specs=out_specs, check_vma=False
    )
```

profile of v0, /device:TPU:0, one launch (start us, length us, event | category | flops | bytes accessed | tf_op | source)
XLA Modules:
  0.0 411.1 jit_solution(6230480748840786355)
XLA Ops:
  7.6 3.6 collective-permute-start
  11.1 1.3 slice.98
  14.5 1.2 fusion.11
  16.0 14.0 %copy.34 = f32[17,16,1024,2]{0,1,3,2:T(8,128)} copy(f32[17,16,1024,2]{2,1,0,3:T(8,128)S(1)} %pad_maximum_fusion.4) | data formatting | bytes 4456448 | tf_op jit(solution)/shard_map/stack | solution.py:31
  30.0 11.5 %slice_bitcast_fusion = f32[17,15,1,2048]{0,1,3,2:T(8,128)} fusion(f32[17,16,2048]{0,1,2:T(8,128)} %bitcast.36), kind=kLoop, calls=%fused_computation.4 | loop fusion | bytes 4177920 | tf_op jit(solution)/shard_map/concatenate | solution.py:82
  41.5 23.0 %copy.42 = bf16[32,32,2048]{1,0,2:T(8,128)(2,1)} copy(bf16[32,32,2048]{2,1,0:T(8,128)(2,1)} %param.5) | data formatting | bytes 8388608 | tf_op args[1]
  64.5 25.0 %gather_fusion = bf16[2048,32,32]{2,1,0:T(8,128)(2,1)} fusion(bf16[32,32,2048]{1,0,2:T(8,128)(2,1)} %copy.42, s32[2048]{0:T(1024)S(1)} %fusion.14), kind=kCustom, calls=%fused_computation | custom fusion | bytes 8396800 | tf_op jit(solution)/shard_map/jit(_take)/gather | solution.py:83
  89.6 17.5 %copy.43 = bf16[2048,32,32]{0,2,1:T(8,128)(2,1)} copy(bf16[2048,32,32]{2,1,0:T(8,128)(2,1)} %gather_fusion) | data formatting | bytes 8388608 | tf_op jit(solution)/shard_map/jit(_take)/gather | solution.py:83
  107.8 11.8 %fusion = f32[17,16,1,2048]{0,1,3,2:T(8,128)S(1)} fusion(f32[17,1,1,2048]{0,1,3,2:T(1,128)S(1)} %bitcast.42, f32[17,15,1,2048]{0,1,3,2:T(8,128)} %slice_bitcast_fusion, f32[17,16,1,2048]{0,1,3,2:T(8,128)} %bitcast.37), kind=kLoop, calls=%fused_computation.6 | loop fusion | flops 1671168 | bytes 6684672 | tf_op jit(solution)/shard_map/mul | solution.py:37
  119.6 36.2 %slice_maximum_fusion = (f32[16,16,2,2048]{0,1,3,2:T(8,128)}, f32[16,16,2,2048]{0,1,3,2:T(8,128)}) fusion(f32[17,16,1,2048]{0,1,3,2:T(8,128)S(1)} %fusion, f32[17,16,1,2048]{0,1,3,2:T(8,128)} %bitcast.38), kind=kLoop, calls=%fused_computation.2 | loop fusion | flops 2097152 | bytes 12845056 | tf_op jit(solution)/shard_map/stack | solution.py:38
  155.8 20.6 %copy.39 = f32[16,16,2,2048]{3,0,2,1:T(8,128)} copy(f32[16,16,2,2048]{0,1,3,2:T(8,128)} %get-tuple-element.11) | data formatting | bytes 8388608 | tf_op jit(solution)/shard_map/slice | solution.py:45
  176.4 20.6 %copy.40 = f32[16,16,2,2048]{3,0,2,1:T(8,128)} copy(f32[16,16,2,2048]{0,1,3,2:T(8,128)} %get-tuple-element.12) | data formatting | bytes 8388608 | tf_op jit(solution)/shard_map/slice | solution.py:44
  197.0 4.4 %fusion.6 = f32[16,1,32,2048]{3,0,2,1:T(8,128)S(1)} fusion(f32[16,1,32,2048]{3,0,2,1:T(8,128)} %bitcast.41, f32[16,1,32,2048]{3,0,2,1:T(8,128)} %bitcast.39), kind=kLoop, calls=%fused_computation.23 | loop fusion | flops 2097152 | bytes 12582912 | tf_op jit(solution)/shard_map/mul | solution.py:44
  202.7 8.1 %copy.41 = f32[16,2,32,2048]{3,2,1,0:T(8,128)} copy(f32[16,2,32,2048]{3,0,2,1:T(8,128)S(1)} %pad_maximum_fusion.3) | data formatting | bytes 16777216 | tf_op jit(solution)/shard_map/stack | solution.py:45
  210.8 4.7 %bitcast_add_fusion = f32[32,32,2048]{2,1,0:T(8,128)S(1)} fusion(f32[16,2,32,2048]{3,2,1,0:T(8,128)} %copy.41, bf16[2048,32,32]{0,2,1:T(8,128)(2,1)S(1)} %copy-done.2, pred[2048]{0:T(1024)(128)(4,1)S(1)} %compare_and_fusion), kind=kLoop, calls=%fused_computation.18 | loop fusion | flops 6291456 | bytes 20973568 | tf_op jit(solution)/shard_map/add | solution.py:83
  215.5 7.7 %fusion.19 = (f32[32,32,2047]{2,1,0:T(8,128)}, f32[32,32,2047]{2,1,0:T(8,128)}) fusion(f32[32,32,2048]{2,1,0:T(8,128)S(1)} %bitcast_add_fusion), kind=kLoop, calls=%fused_computation.49 | loop fusion | bytes 33538048 | tf_op jit(solution)/shard_map/jit(_roll_static)/slice | solution.py:51
  223.3 6.1 %fusion.22 = (f32[31,32,2048]{2,1,0:T(8,128)}, f32[31,32,2048]{2,1,0:T(8,128)}) fusion(f32[32,32,2048]{2,1,0:T(8,128)S(1)} %bitcast_add_fusion), kind=kLoop, calls=%fused_computation.52 | loop fusion | bytes 32505856 | tf_op jit(solution)/shard_map/slice | solution.py:53
  230.8 3.7 collective-permute-done.1
  234.5 3.1 collective-permute-done.2
  237.6 37.9 %multiply_reduce_fusion.1 = (f32[32,2048]{1,0:T(8,128)S(1)}, f32[32,2048]{1,0:T(8,128)S(1)}, f32[32,2048]{1,0:T(8,128)S(1)}, f32[32,2048]{1,0:T(8,128)S(1)}) fusion(f32[32,32,2048]{2,1,0:T(8,128)} %copy-done, f32[31,32,2048]{2,1,0:T(8,128)} %get-tuple-element.20, f32[1,32,2048]{2,1,0:T(8,128)S(1)} %get-tuple-element.22, ...), kind=kOutput, calls=%fused_computation.20 | output fusion | flops 203161600 | bytes 43515904 | tf_op jit(solution)/shard_map/jit(cumsum)/reduce_window_sum | solution.py:61
  277.6 49.2 %all-gather.3.cloned.1.call-done = f32[512,2048]{1,0:T(8,128)} async-done(((f32[32,2048]{1,0:T(8,128)}), f32[512,2048]{1,0:T(8,128)}) %all-gather.3.cloned.1.call-update) | async-done | bytes 4194320 | tf_op jit(solution)/shard_map/all_gather | solution.py:90
  326.8 2.8 select_reduce_fusion
  330.5 72.3 %reduce-scatter.2.cloned.1.call-done = f32[3,32,128]{2,1,0:T(8,128)} async-done(((f32[3,32,2048]{2,1,0:T(8,128)}), f32[3,32,128]{2,1,0:T(8,128)}) %reduce-scatter.2.cloned.1.call-update) | async-done | bytes 49168 | tf_op jit(solution)/shard_map/reduce_scatter | solution.py:95
  402.9 1.4 pad_maximum_fusion.6
  (39 shorter events, 9.8 us)
Async XLA Ops:
  6.5 320.2 %all-gather.3.cloned.1.call-start = ((), (), s32[]{:S(2)}) async-start(), calls=%async_computation.2 | async-start | bytes 4456448 | tf_op jit(solution)/shard_map/all_gather | solution.py:90
  7.6 99.5 %collective-permute-start = (bf16[17,1,1024]{2,0,1:T(8,128)(2,1)S(1)}, bf16[17,1,1024]{2,0,1:T(8,128)(2,1)S(1)}, u32[]{:S(2)}, u32[]{:S(2)}) collective-permute-start(bf16[17,1,1024]{2,0,1:T(8,128)(2,1)S(1)} %copy.44), channel_id=1, source_target_pairs={{0,7},{1,0},{2,1},{3,2},{4,3},{5,4},{6,5},{7,6},{8,15},{9,8},{10,9... | collective-permute-start | bytes 104456 | tf_op jit(solution)/shard_map/ppermute | solution.py:9
  30.0 11.5 %copy-start.3 = (s32[2048]{0:T(1024)S(1)}, s32[2048]{0:T(1024)}, u32[]{:S(2)}) copy-start(s32[2048]{0:T(1024)} %param.6) | copy-start | bytes 24580
  197.0 4.6 %copy-start.1 = (f32[16,16,2,2048]{3,0,2,1:T(8,128)S(1)}, f32[16,16,2,2048]{3,0,2,1:T(8,128)}, u32[]{:S(2)}) copy-start(f32[16,16,2,2048]{3,0,2,1:T(8,128)} %copy.39) | copy-start | bytes 12582916
  202.7 8.1 %copy-start.2 = (bf16[2048,32,32]{0,2,1:T(8,128)(2,1)S(1)}, bf16[2048,32,32]{0,2,1:T(8,128)(2,1)}, u32[]{:S(2)}) copy-start(bf16[2048,32,32]{0,2,1:T(8,128)(2,1)} %copy.43) | copy-start | bytes 12582916
  215.5 15.0 %copy-start = (f32[32,32,2048]{2,1,0:T(8,128)}, f32[32,32,2048]{2,1,0:T(8,128)S(1)}, u32[]{:S(2)}) copy-start(f32[32,32,2048]{2,1,0:T(8,128)S(1)} %bitcast_add_fusion) | copy-start | bytes 25165828
  229.9 4.6 %collective-permute-start.1 = (f32[32,1,2048]{2,1,0:T(1,128)S(1)}, f32[32,1,2048]{2,1,0:T(1,128)S(1)}, u32[]{:S(2)}, u32[]{:S(2)}) collective-permute-start(f32[32,1,2048]{2,1,0:T(1,128)S(1)} %get-tuple-element.17), channel_id=1, source_target_pairs={{1,0},{2,1},{3,2},{4,3},{5,4},{6,5},{7,6},{0,7},{9,8},{10,9},{11,1... | collective-permute-start | bytes 786440 | tf_op jit(solution)/shard_map/ppermute | solution.py:21
  230.6 7.0 %collective-permute-start.2 = (f32[32,1,2048]{2,1,0:T(1,128)S(1)}, f32[32,1,2048]{2,1,0:T(1,128)S(1)}, u32[]{:S(2)}, u32[]{:S(2)}) collective-permute-start(f32[32,1,2048]{2,1,0:T(1,128)S(1)} %get-tuple-element.18), channel_id=1, source_target_pairs={{0,1},{1,2},{2,3},{3,4},{4,5},{5,6},{6,7},{7,0},{8,9},{9,10},{10,1... | collective-permute-start | bytes 786440 | tf_op jit(solution)/shard_map/ppermute | solution.py:19
  237.6 38.8 %copy-start.4 = (s32[16]{0:T(128)S(1)}, s32[16]{0:T(128)}, u32[]{:S(2)}) copy-start(s32[16]{0:T(128)} %param.7) | copy-start | bytes 196
  276.3 126.6 %reduce-scatter.2.cloned.1.call-start = ((), (), s32[]{:S(2)}) async-start(), calls=%async_computation.1 | async-start | bytes 835584 | tf_op jit(solution)/shard_map/reduce_scatter | solution.py:95
Sparse Core Ops, SparseCore 0:
  276.4 50.2 all-gather.2
  330.6 72.1 reduce-scatter.1
where the time goes:
time: 413 us; the launch traced here: 411 us
  local copies, waits for them, and re-layouts  159 us (38%)
  waiting for transfers between devices  128 us (31%)
  other arithmetic  105 us (25%)
  between operations  13.6 us (3%)
  starting transfers between devices  4.31 us (1%)
    reduce_scatter x1, waiting for transfers between devices, on_device(): lax.psum_scatter(nearer[None] * shaded, 'depth', scatter_dimension=2, til...  72.3 us
    all_gather x1, waiting for transfers between devices, on_device(): pieces_here = lax.all_gather(through[None], 'depth', axis=0, tiled=True)  49.2 us
    gather x2, local copies, waits for them, and re-layouts, on_device(): jnp.take(detail, layout, axis=2).astype(jnp.float32)  42.5 us
    another operation x1, other arithmetic, shade_brick(): before = jnp.cumsum(optical, axis=0) - optical  37.9 us
    another operation x1, other arithmetic, lengthen(): jnp.stack([coarse_vals, midway], axis=2)  36.2 us
    unnamed x12, local copies, waits for them, and re-layouts  23.3 us
    slice x1, local copies, waits for them, and re-layouts, deepen(): coarse_vals[:-1]  20.6 us
    slice x1, local copies, waits for them, and re-layouts, deepen(): midway = 0.5 * (coarse_vals[:-1] + coarse_vals[1:])  20.6 us
  transfers between devices with their start and end apart: 5, of which 4 were waited for; matrix products, arithmetic and copies ran while one was open for 24% of the time, Pallas kernels for 0%

commit v1 on v0

v1 whole, which is shorter than its diff:
```python
import functools
import math

import jax
import jax.numpy as jnp
from jax import lax
from jax.experimental import pallas as pl
from jax.experimental.pallas import tpu as pltpu
from jax.sharding import PartitionSpec as P

F32 = jnp.float32
BF16 = jnp.bfloat16
BLOCKS = 16
TILES = 8
PLANES = 32
PITCH = 40
CPITCH = 24
LOG2E = math.log2(math.e)
GAIN = 0.65 * 0.48
STEPS = 2048.0
COLOR_TOP = 32767.0
TAU_TOP = 32767.0 - 10 * 2048.0


def fit_weight():
    import numpy as np

    top = 0.0545
    k = np.cos(np.pi * (np.arange(64) + 0.5) / 64)
    o = (k + 1) * top / 2
    c = np.polynomial.chebyshev.chebfit(k, -np.expm1(-o) / o, 2)
    p = np.polynomial.chebyshev.cheb2poly(c)
    q = np.zeros(3)
    base = np.poly1d([2 / top, -1.0])
    poly = np.poly1d([0.0])
    for i, ci in enumerate(p):
        poly = poly + ci * base**i
    q[: len(poly.coeffs)] = poly.coeffs[::-1]
    kappa = math.log(2) / 256
    return tuple(float(q[i] * kappa ** (i + 1)) for i in range(3))


W0, W1, W2 = fit_weight()


def onehot(lay_ref, p_ref, t):
    lay = lay_ref[pl.ds(t, 1), :]
    hi = lay // 256
    lo = lay - hi * 256
    rows = lax.broadcasted_iota(jnp.int32, (256, 256), 0).astype(BF16)
    for a in range(8):
        key = jnp.where(hi == a, lo, -1).astype(BF16)
        p_ref[256 * a : 256 * a + 256, :] = jnp.where(rows == key, BF16(1), BF16(0))


def coarse_tile(t, coarse_ref, ctop_ref, cbot_ref, w_ref, c_ref, h_ref):
    k0 = pl.multiple_of(t * 128, 128)
    k1 = pl.multiple_of(jnp.where(t == 7, 0, t + 1) * 128, 128)

    def widened(ref):
        both = jnp.concatenate([ref[:, pl.ds(k0, 128)], ref[:, pl.ds(k1, 128)]], axis=1)
        return jnp.dot(both, w_ref[...], preferred_element_type=F32)

    own, top, bot = widened(coarse_ref), widened(ctop_ref), widened(cbot_ref)
    for b in range(2):
        cols = slice(128 * b, 128 * b + 128)
        for m in range(17):
            c_ref[b, CPITCH * m + 8 : CPITCH * m + 24, :] = own[16 * m : 16 * m + 16, cols]
        for m in range(0, 24, 8):
            c_ref[b, pl.ds(CPITCH * m + 7, 8, stride=CPITCH), :] = top[m : m + 8, cols]
            c_ref[b, pl.ds(CPITCH * (m + 1), 8, stride=CPITCH), :] = bot[m : m + 8, cols]
        for m in range(17):
            for a in range(2):
                near = c_ref[b, CPITCH * m + 8 + 8 * a : CPITCH * m + 16 + 8 * a, :]
                far = c_ref[b, CPITCH * m + 9 + 8 * a : CPITCH * m + 17 + 8 * a, :]
                h_ref[b, pl.ds(PITCH * m + 8 + 16 * a, 8, stride=2), :] = near + near
                h_ref[b, pl.ds(PITCH * m + 9 + 16 * a, 8, stride=2), :] = near + far
        for m in range(0, 24, 8):
            edge = c_ref[b, pl.ds(CPITCH * m + 7, 8, stride=CPITCH), :]
            first = c_ref[b, pl.ds(CPITCH * m + 8, 8, stride=CPITCH), :]
            last = c_ref[b, pl.ds(CPITCH * (m + 1), 8, stride=CPITCH), :]
            h_ref[b, pl.ds(PITCH * m + 7, 8, stride=PITCH), :] = edge + first
            h_ref[b, pl.ds(PITCH * (m + 1), 8, stride=PITCH), :] = last + last


def values_tile(t, d_ref, h_ref, v_ref):
    for b in range(2):
        block = 2 * t + b
        cols = slice(128 * b, 128 * b + 128)
        for z in range(PLANES):
            m, n = z // 2, (z + 1) // 2
            at = PITCH * z + 8
            for g in range(0, 32, 8):
                near = h_ref[b, PITCH * m + 8 + g : PITCH * m + 16 + g, :]
                far = near if n == m else h_ref[b, PITCH * n + 8 + g : PITCH * n + 16 + g, :]
                v_ref[block, at + g : at + g + 8, :] = d_ref[32 * z + g : 32 * z + g + 8, cols] + (near + far)
        for side, row in ((0, 7), (1, PITCH)):
            for odd in range(2):
                for m in range(0, 16, 8):
                    near = h_ref[b, pl.ds(PITCH * m + row, 8, stride=PITCH), :]
                    far = near if odd == 0 else h_ref[b, pl.ds(PITCH * (m + 1) + row, 8, stride=PITCH), :]
                    r = 1024 + 32 * side + 16 * odd + m
                    v_ref[block, pl.ds(PITCH * (2 * m + odd) + row, 8, stride=2 * PITCH), :] = d_ref[r : r + 8, cols] + (near + far)


def matmul_tile(a_ref, e_ref, p_ref, d_ref):
    d_ref[0:1024, :] = jnp.dot(a_ref[...], p_ref[...], preferred_element_type=F32)
    d_ref[1024:1088, :] = jnp.dot(e_ref[...], p_ref[...], preferred_element_type=F32)


def code(x, top):
    c = jnp.floor(jnp.log2(x) * STEPS + (top + 0.5))
    return jnp.minimum(jnp.maximum(c, -32768.0), 32767.0)


def march(v_ref, block, g):
    lane = lax.broadcasted_iota(jnp.int32, (8, 128), 1)
    first, last = lane == 0, lane == 127
    left = jnp.where(block == 0, BLOCKS - 1, block - 1)
    right = jnp.where(block == BLOCKS - 1, 0, block + 1)

    def load(of, z, off=0):
        at = PITCH * z + 8 + 8 * g + off
        return v_ref[of, at : at + 8, :]

    zero = jnp.zeros((8, 128), F32)
    c = prev = load(block, 0)
    through = zero + 1.0
    a0 = a1 = a2 = a3 = zero
    for z in range(PLANES):
        following = load(block, z + 1) if z + 1 < PLANES else c
        xp = pltpu.roll(jnp.where(first, load(right, z), c), 127, 1)
        xm = pltpu.roll(jnp.where(last, load(left, z), c), 1, 1)
        dx = xp - xm
        dy = load(block, z, 1) - load(block, z, -1)
        dz = following - prev
        along = dx + (0.6 / 0.48) * dy + (0.64 / 0.48) * dz
        square = (4.0 + dx * dx) + (dy * dy + dz * dz)
        shading = 0.35 / GAIN + jnp.abs(along) * lax.rsqrt(square)
        l = jnp.log2(1.0 + jnp.exp2(c * (1.5 * LOG2E) - 0.5 * LOG2E))
        weight = through * (l * (W0 + l * (W1 + l * W2)))
        through = through - weight
        ws = weight * shading
        a0 = a0 + ws
        a1 = a1 + ws * jnp.tanh(c)
        a2 = a2 + ws * jnp.tanh(0.5 * c)
        a3 = a3 + ws * jnp.exp2((c * c) * (-0.5 * LOG2E))
        prev, c = c, following
    return a0, a1, a2, a3, through


def march_block(v_ref, o_ref, block):
    for half in range(2):
        sets = []
        for g in (2 * half, 2 * half + 1):
            a0, a1, a2, a3, through = march(v_ref, block, g)
            sets.append(
                (
                    code((0.5 * GAIN) * (a0 + a1), COLOR_TOP),
                    code((0.5 * GAIN) * (a0 - a2), COLOR_TOP),
                    code(GAIN * a3, COLOR_TOP),
                    code(-jnp.log2(through), TAU_TOP),
                )
            )
        for i in range(4):
            both = jnp.concatenate([sets[0][i], sets[1][i]], 0)
            o_ref[block, i, 16 * half : 16 * half + 16, :] = both.astype(jnp.int32).astype(jnp.int16)


def brick_kernel(a_ref, e_ref, coarse_ref, ctop_ref, cbot_ref, w_ref, lay_ref, o_ref, v_ref, p_ref, d_ref, c_ref, h_ref):
    def finish(t):
        coarse_tile(t, coarse_ref, ctop_ref, cbot_ref, w_ref, c_ref, h_ref)
        values_tile(t, d_ref, h_ref, v_ref)

    def early(i, _):
        t = jnp.where(i == 0, TILES - 1, 0)
        onehot(lay_ref, p_ref, t)
        matmul_tile(a_ref, e_ref, p_ref, d_ref)
        finish(t)
        return 0

    lax.fori_loop(0, 2, early, 0)
    onehot(lay_ref, p_ref, 1)

    def step(s, _):
        matmul_tile(a_ref, e_ref, p_ref, d_ref)
        march_block(v_ref, o_ref, jnp.where(s == 0, BLOCKS - 1, 2 * s - 1))
        march_block(v_ref, o_ref, 2 * s)
        finish(s + 1)
        onehot(lay_ref, p_ref, jnp.minimum(s + 2, TILES - 1))
        return 0

    lax.fori_loop(0, 6, step, 0)

    def late(s, _):
        march_block(v_ref, o_ref, 2 * s - 1)
        march_block(v_ref, o_ref, 2 * s)
        return 0

    lax.fori_loop(6, 8, late, 0)


def widening():
    import numpy as np

    w = np.zeros((256, 256), np.float32)
    for j in range(129):
        for x, part in ((2 * j, 0.25), (2 * j + 1, 0.125), (2 * j - 1, 0.125)):
            if 0 <= x < 256:
                w[j, x] = part
    return jnp.asarray(w, BF16)


VMEM = pl.BlockSpec(memory_space=pltpu.VMEM)


def brick(a, e, coarse, ctop, cbot, lay):
    return pl.pallas_call(
        brick_kernel,
        out_shape=jax.ShapeDtypeStruct((BLOCKS, 4, 32, 128), jnp.int16),
        in_specs=[VMEM] * 7,
        out_specs=VMEM,
        scratch_shapes=[
            pltpu.VMEM((BLOCKS, 33 * PITCH, 128), F32),
            pltpu.VMEM((2048, 256), BF16),
            pltpu.VMEM((1088, 256), F32),
            pltpu.VMEM((2, 25 * CPITCH, 128), F32),
            pltpu.VMEM((2, 25 * PITCH, 128), F32),
        ],
        compiler_params=pltpu.CompilerParams(vmem_limit_bytes=56 * 2**20),
        name="brick",
    )(a, e, coarse, ctop, cbot, widening(), lay)


def composite_kernel(order_ref, parts_ref, o_ref):
    flip = order_ref[0]

    def image(b, i):
        x = parts_ref[b, i].astype(jnp.int32).astype(F32)
        top = TAU_TOP if i == 3 else COLOR_TOP
        return jnp.where(x > -32768.0, jnp.exp2((x - top) * (1.0 / STEPS)), 0.0)

    tau = jnp.zeros((32, 128), F32)
    sums = [jnp.zeros((32, 128), F32) for _ in range(3)]
    for rank in range(BLOCKS):
        b = rank ^ flip
        passing = jnp.exp2(-tau)
        for i in range(3):
            sums[i] = sums[i] + passing * image(b, i)
        tau = tau + image(b, 3)
    for i in range(3):
        o_ref[i] = sums[i]
    o_ref[3] = 1.0 - jnp.exp2(-tau)


def composite(order, parts):
    return pl.pallas_call(
        composite_kernel,
        out_shape=jax.ShapeDtypeStruct((4, 32, 128), F32),
        in_specs=[pl.BlockSpec(memory_space=pltpu.SMEM), VMEM],
        out_specs=VMEM,
        name="composite",
    )(order, parts)


def edge(detail, coarse, row, crow):
    lines = detail[:, row, :]
    fine = jnp.concatenate([lines[0::2], lines[1::2]], 0)
    rough = jnp.pad(coarse[:, crow, :], ((0, 15), (0, 0)))
    return jnp.concatenate([fine, rough], 1)


def on_device(coarse, detail, layout, view_order):
    n = lax.axis_size("rows")
    above = lax.ppermute(edge(detail, coarse, 31, 15), "rows", [(i, (i + 1) % n) for i in range(n)])
    below = lax.ppermute(edge(detail, coarse, 0, 0), "rows", [((i + 1) % n, i) for i in range(n)])
    halo = jnp.concatenate([above[:, :2048], below[:, :2048]], 0)
    codes = brick(
        detail.reshape(1024, 2048), halo, coarse.reshape(272, 1024), above[:, 2048:], below[:, 2048:], layout.reshape(8, 256)
    )
    parts = lax.all_to_all(codes, "depth", 0, 0, tiled=True)
    return composite(view_order, parts)


def solution(mesh):
    in_specs = (P("depth", "rows", None), P("depth", "rows", None), P(), P())
    out_specs = P(None, "rows", "depth")
    return jax.shard_map(on_device, mesh=mesh, in_specs=in_specs, out_specs=out_specs, check_vma=False)
```

time: 413 us -> 60.8 us (0.15)
  local copies, waits for them, and re-layouts: 159 us -> 6.11 us
  waiting for transfers between devices: 128 us -> 1.88 us
  other arithmetic: 105 us -> 0.75 us
  Pallas kernels: 0 us -> 28.8 us
  blocking collectives: 0 us -> 19.3 us
  between operations: 13.6 us -> 0.08 us
    another operation x9 -> x0, other arithmetic: 78 us -> none  [the longest x1 37.9 us: shade_brick(): before = jnp.cumsum(optical, axis=0) - optical]
    reduce_scatter x1 -> x0, waiting for transfers between devices: 72.3 us -> none  [on_device(): lax.psum_scatter(nearer[None] * shaded, 'depth', scatter_dimension=2, til...]
    slice x12 -> x10, local copies, waits for them, and re-layouts: 59 us -> 4.63 us  [the longest x1 1.97 us: edge(): lines = detail[:, row, :]]
    all_gather x1 -> x0, waiting for transfers between devices: 49.2 us -> none  [on_device(): pieces_here = lax.all_gather(through[None], 'depth', axis=0, tiled=True)]
    gather x2 -> x0, local copies, waits for them, and re-layouts: 42.5 us -> none  [on_device(): jnp.take(detail, layout, axis=2).astype(jnp.float32)]
    pallas_call x0 -> x2, Pallas kernels: none -> 28.8 us  [the longest x1 26.8 us: brick(): pl.pallas_call(brick_kernel, out_shape=jax.ShapeDtypeStruct((BLOCKS, 4, 3...]
    unnamed x12 -> x2, local copies, waits for them, and re-layouts: 23.3 us -> 0.03 us
    another operation x3 -> x0, local copies, waits for them, and re-layouts: 22.6 us -> none  [the longest x2 14.5 us: widen_cols(): jnp.stack([coarse_vals, midway], axis=-1)]
  transfers between devices with their start and end apart: 5 -> 2, of which waited for: 4 -> 1; matrix products, arithmetic and copies ran while one was open for 24% -> 2% of each run, Pallas kernels for 0% -> 0%
where the time goes in v1:
time: 60.8 us; the launch traced here: 60.5 us
  Pallas kernels  28.8 us (47%)
  blocking collectives  19.3 us (32%)
  local copies, waits for them, and re-layouts  6.11 us (10%)
  starting transfers between devices  3.59 us (6%)
  waiting for transfers between devices  1.88 us (3%)
  other arithmetic  0.75 us (1%)
    pallas_call x1, Pallas kernels, brick(): pl.pallas_call(brick_kernel, out_shape=jax.ShapeDtypeStruct((BLOCKS, 4, 3...  26.8 us
    all_to_all x1, blocking collectives, on_device(): parts = lax.all_to_all(codes, 'depth', 0, 0, tiled=True)  19.3 us
    ppermute x1, starting transfers between devices, on_device(): lax.ppermute(edge(detail, coarse, 0, 0), 'rows', [((i + 1) % n, i) for i...  3.57 us
    pallas_call x1, Pallas kernels, composite(): pl.pallas_call(composite_kernel, out_shape=jax.ShapeDtypeStruct((4, 32, 1...  2 us
    slice x1, local copies, waits for them, and re-layouts, edge(): lines = detail[:, row, :]  1.97 us
    ppermute x1, waiting for transfers between devices, on_device(): lax.ppermute(edge(detail, coarse, 31, 15), 'rows', [(i, (i + 1) % n) for...  1.87 us
    reshape x1, local copies, waits for them, and re-layouts, on_device(): layout.reshape(8, 256)  1.29 us
  transfers between devices with their start and end apart: 2, of which 1 were waited for; matrix products, arithmetic and copies ran while one was open for 2% of the time, Pallas kernels for 0%

profile of v1, /device:TPU:0, one launch (start us, length us, event | category | flops | bytes accessed | tf_op | source)
XLA Modules:
  0.0 60.5 jit_solution(11291966105389411984)
XLA Ops:
  0.0 2.0 %fusion.4 = (bf16[32,1,2048]{2,1,0:T(2,128)(2,1)S(1)}, bf16[32,1,2048]{2,1,0:T(2,128)(2,1)S(1)}) fusion(bf16[32,32,2048]{2,1,0:T(8,128)(2,1)} %param.6), kind=kLoop, calls=%fused_computation.10 | loop fusion | bytes 524288 | tf_op jit(solution)/shard_map/slice | solution.py:267
  2.0 0.2 copy_bitcast_fusion
  2.1 0.1 slice.38
  2.2 0.1 slice.37
  2.3 1.2 %fusion.5 = (bf16[17,1,1024]{2,1,0:T(2,128)(2,1)S(1)}, bf16[17,1,1024]{2,1,0:T(2,128)(2,1)S(1)}) fusion(bf16[17,16,1024]{2,1,0:T(8,128)(2,1)} %param.5), kind=kLoop, calls=%fused_computation.11 | loop fusion | bytes 139264 | tf_op jit(solution)/shard_map/slice | solution.py:269
  3.5 0.0 collective-permute-start
  3.5 0.1 slice.43
  3.5 0.1 slice.42
  3.7 3.6 %collective-permute-start.1 = (bf16[32,3072]{1,0:T(8,128)(2,1)S(1)}, bf16[32,3072]{1,0:T(8,128)(2,1)S(1)}, u32[]{:S(2)}, u32[]{:S(2)}) collective-permute-start(bf16[32,3072]{1,0:T(8,128)(2,1)S(1)} %fusion.3), channel_id=1, source_target_pairs={{1,0},{2,1},{3,2},{4,3},{5,4},{6,5},{7,6},{0,7},{9,8},{10,9},{11,1... | collective-permute-start | bytes 589832 | tf_op jit(solution)/shard_map/ppermute | solution.py:276
  7.2 1.3 %reshape.11.lay_ref = s32[8,256]{1,0:T(8,128)} reshape(s32[2048]{0:T(1024)} %param.7) | data formatting | bytes 16384 | tf_op jit(solution)/shard_map/reshape | solution.py:279
  8.5 1.9 %collective-permute-done = bf16[32,3072]{1,0:T(8,128)(2,1)S(1)} collective-permute-done((bf16[32,3072]{1,0:T(8,128)(2,1)S(1)}, bf16[32,3072]{1,0:T(8,128)(2,1)S(1)}, u32[]{:S(2)}, u32[]{:S(2)}) %collective-permute-start) | collective-permute-done | bytes 196640 | tf_op jit(solution)/shard_map/ppermute | solution.py:275
  10.4 0.0 collective-permute-done.1
  10.4 0.7 %pad_maximum_fusion.e_ref = bf16[64,2048]{1,0:T(8,128)(2,1)} fusion(bf16[32,2048]{1,0:T(8,128)(2,1)S(1)} %slice.49, bf16[32,2048]{1,0:T(8,128)(2,1)S(1)} %slice.48), kind=kLoop, calls=%fused_computation.3 | loop fusion | flops 524288 | bytes 524288 | tf_op jit(solution)/shard_map/concatenate | solution.py:277
  11.1 0.6 %slice.50.ctop_ref = bf16[32,1024]{1,0:T(8,128)(2,1)} slice(bf16[32,3072]{1,0:T(8,128)(2,1)S(1)} %collective-permute-done), slice={[0:32], [2048:3072]} | slice | bytes 131072 | tf_op jit(solution)/shard_map/slice | solution.py:279
  11.8 0.6 %slice.51.cbot_ref = bf16[32,1024]{1,0:T(8,128)(2,1)} slice(bf16[32,3072]{1,0:T(8,128)(2,1)S(1)} %collective-permute-done.1), slice={[0:32], [2048:3072]} | slice | bytes 131072 | tf_op jit(solution)/shard_map/slice | solution.py:279
  12.4 26.8 %brick.1 = s16[16,4,32,128]{3,2,1,0:T(8,128)(2,1)} custom-call(bf16[1024,2048]{1,0:T(8,128)(2,1)} %bitcast.12, bf16[64,2048]{1,0:T(8,128)(2,1)} %pad_maximum_fusion.e_ref, bf16[272,1024]{1,0:T(8,128)(2,1)} %bitcast.13, bf16[32,1024]{1,0:T(8,128)(2,1)} %slice.50.ctop_ref, bf16[32,1024]{1,0:T(8,128)(2,1)} %slice.51.cbot_ref, ...), custom_call_target="tpu_custom_call" | custom-call | tf_op jit(solution)/shard_map/brick/pallas_call | solution.py:218
  39.2 19.3 %all_to_all.5.parts_ref = s16[16,4,32,128]{3,2,1,0:T(8,128)(2,1)} all-to-all(s16[16,4,32,128]{3,2,1,0:T(8,128)(2,1)} %brick.1), channel_id=1, replica_groups=mesh['depth'=16,'rows'=8] {'depth'}, dimensions={0} | all-to-all | bytes 1048576 | tf_op jit(solution)/shard_map/all_to_all | solution.py:281
  58.5 2.0 %composite.1 = f32[4,32,128]{2,1,0:T(8,128)} custom-call(s32[16]{0:T(128)} %order_ref.1, s16[16,4,32,128]{3,2,1,0:T(8,128)(2,1)} %all_to_all.5.parts_ref), custom_call_target="tpu_custom_call" | custom-call | tf_op jit(solution)/shard_map/composite/pallas_call | solution.py:257
  (6 shorter events, 0.1 us)
Async XLA Ops:
  3.5 6.9 %collective-permute-start = (bf16[32,3072]{1,0:T(8,128)(2,1)S(1)}, bf16[32,3072]{1,0:T(8,128)(2,1)S(1)}, u32[]{:S(2)}, u32[]{:S(2)}) collective-permute-start(bf16[32,3072]{1,0:T(8,128)(2,1)S(1)} %fusion.2), channel_id=1, source_target_pairs={{0,1},{1,2},{2,3},{3,4},{4,5},{5,6},{6,7},{7,0},{8,9},{9,10},{10,1... | collective-permute-start | bytes 589832 | tf_op jit(solution)/shard_map/ppermute | solution.py:275
  3.7 6.8 %collective-permute-start.1 = (bf16[32,3072]{1,0:T(8,128)(2,1)S(1)}, bf16[32,3072]{1,0:T(8,128)(2,1)S(1)}, u32[]{:S(2)}, u32[]{:S(2)}) collective-permute-start(bf16[32,3072]{1,0:T(8,128)(2,1)S(1)} %fusion.3), channel_id=1, source_target_pairs={{1,0},{2,1},{3,2},{4,3},{5,4},{6,5},{7,6},{0,7},{9,8},{10,9},{11,1... | collective-permute-start | bytes 589832 | tf_op jit(solution)/shard_map/ppermute | solution.py:276

commit v2 on v1

v2 whole, which is shorter than its diff:
```python
import functools
import math

import jax
import jax.numpy as jnp
from jax import lax
from jax.experimental import pallas as pl
from jax.experimental.pallas import tpu as pltpu
from jax.sharding import PartitionSpec as P

F32 = jnp.float32
BF16 = jnp.bfloat16
BLOCKS = 16
TILES = 8
PLANES = 32
HALF = 544
PITCH = 40
CPITCH = 24
LOG2E = math.log2(math.e)
GAIN = 0.65 * 0.48
STEPS = 2048.0
COLOR_TOP = 32767.0
TAU_TOP = 32767.0 - 10 * 2048.0


def fit_weight():
    import numpy as np

    top = 0.0545
    k = np.cos(np.pi * (np.arange(64) + 0.5) / 64)
    o = (k + 1) * top / 2
    c = np.polynomial.chebyshev.chebfit(k, -np.expm1(-o) / o, 2)
    p = np.polynomial.chebyshev.cheb2poly(c)
    q = np.zeros(3)
    base = np.poly1d([2 / top, -1.0])
    poly = np.poly1d([0.0])
    for i, ci in enumerate(p):
        poly = poly + ci * base**i
    q[: len(poly.coeffs)] = poly.coeffs[::-1]
    kappa = math.log(2) / 256
    return tuple(float(q[i] * kappa ** (i + 1)) for i in range(3))


W0, W1, W2 = fit_weight()


def onehot(lay_ref, p_ref, at, t):
    lay = lay_ref[pl.ds(t, 1), :]
    hi = lay // 256
    lo = lay - hi * 256
    rows = lax.broadcasted_iota(jnp.int32, (256, 256), 0).astype(BF16)
    for a in range(8):
        key = jnp.where(hi == a, lo, -1).astype(BF16)
        p_ref[at, 256 * a : 256 * a + 256, :] = jnp.where(rows == key, BF16(1), BF16(0))


def coarse_tile(t, k_ref, w_ref, c_ref, h_ref):
    k0 = pl.multiple_of(t * 128, 128)
    k1 = pl.multiple_of((t + 1) % 8 * 128, 128)
    both = jnp.concatenate([k_ref[:, pl.ds(k0, 128)], k_ref[:, pl.ds(k1, 128)]], axis=1)
    wide = jnp.dot(both, w_ref[...], preferred_element_type=F32)
    own, top, bot = wide[:272], wide[272:304], wide[304:]
    for b in range(2):
        cols = slice(128 * b, 128 * b + 128)
        for m in range(17):
            c_ref[b, CPITCH * m + 8 : CPITCH * m + 24, :] = own[16 * m : 16 * m + 16, cols]
        for m in range(0, 24, 8):
            c_ref[b, pl.ds(CPITCH * m + 7, 8, stride=CPITCH), :] = top[m : m + 8, cols]
            c_ref[b, pl.ds(CPITCH * (m + 1), 8, stride=CPITCH), :] = bot[m : m + 8, cols]
        for m in range(17):
            for a in range(2):
                near = c_ref[b, CPITCH * m + 8 + 8 * a : CPITCH * m + 16 + 8 * a, :]
                far = c_ref[b, CPITCH * m + 9 + 8 * a : CPITCH * m + 17 + 8 * a, :]
                h_ref[b, pl.ds(PITCH * m + 8 + 16 * a, 8, stride=2), :] = near + near
                h_ref[b, pl.ds(PITCH * m + 9 + 16 * a, 8, stride=2), :] = near + far
        for m in range(0, 24, 8):
            edge = c_ref[b, pl.ds(CPITCH * m + 7, 8, stride=CPITCH), :]
            first = c_ref[b, pl.ds(CPITCH * m + 8, 8, stride=CPITCH), :]
            last = c_ref[b, pl.ds(CPITCH * (m + 1), 8, stride=CPITCH), :]
            h_ref[b, pl.ds(PITCH * m + 7, 8, stride=PITCH), :] = edge + first
            h_ref[b, pl.ds(PITCH * (m + 1), 8, stride=PITCH), :] = last + last


def local_terms(c):
    l = jnp.log2(1.0 + jnp.exp2(c * (1.5 * LOG2E) - 0.5 * LOG2E))
    return l * (W0 + l * (W1 + l * W2)), jnp.tanh(c), jnp.tanh(0.5 * c), jnp.exp2((c * c) * (-0.5 * LOG2E))


def values_tile(d_ref, h_ref, v_ref, e_refs):
    for b in range(2):
        cols = slice(128 * b, 128 * b + 128)
        for z in range(PLANES):
            m, n = z // 2, (z + 1) // 2
            at = PITCH * z + 8
            for g in range(0, 32, 8):
                near = h_ref[b, PITCH * m + 8 + g : PITCH * m + 16 + g, :]
                far = near if n == m else h_ref[b, PITCH * n + 8 + g : PITCH * n + 16 + g, :]
                c = d_ref[32 * z + g : 32 * z + g + 8, cols] + (near + far)
                v_ref[b, at + g : at + g + 8, :] = c
                if e_refs[b] is not None:
                    for i, term in enumerate(local_terms(c)):
                        e_refs[b][i, 32 * z + g : 32 * z + g + 8, :] = term
        for side, row in ((0, 7), (1, PITCH)):
            for odd in range(2):
                for m in range(0, 16, 8):
                    near = h_ref[b, pl.ds(PITCH * m + row, 8, stride=PITCH), :]
                    far = near if odd == 0 else h_ref[b, pl.ds(PITCH * (m + 1) + row, 8, stride=PITCH), :]
                    r = 1024 + 32 * side + 16 * odd + m
                    v_ref[b, pl.ds(PITCH * (2 * m + odd) + row, 8, stride=2 * PITCH), :] = d_ref[r : r + 8, cols] + (near + far)


def matmul_tile(a_ref, p_ref, at, d_ref):
    for r in (0, HALF):
        d_ref[r : r + HALF, :] = jnp.dot(a_ref[r : r + HALF, :], p_ref[at], preferred_element_type=F32)


def code(x, top):
    c = jnp.floor(jnp.log2(x) * STEPS + (top + 0.5))
    return jnp.minimum(jnp.maximum(c, -32768.0), 32767.0)


def march(trio, e_ref, groups):
    before, here, after = trio
    lane = lax.broadcasted_iota(jnp.int32, (8, 128), 1)
    first, last = lane == 0, lane == 127

    def load(of, g, z, off=0):
        at = PITCH * z + 8 + 8 * g + off
        return of[0][of[1], at : at + 8, :]

    zero = jnp.zeros((8, 128), F32)
    state = []
    for g in groups:
        c = load(here, g, 0)
        state.append((c, c, zero + 1.0, zero, zero, zero, zero))
    for z in range(PLANES):
        for at, g in enumerate(groups):
            prev, c, through, a0, a1, a2, a3 = state[at]
            following = load(here, g, z + 1) if z + 1 < PLANES else c
            xp = pltpu.roll(jnp.where(first, load(after, g, z), c), 127, 1)
            xm = pltpu.roll(jnp.where(last, load(before, g, z), c), 1, 1)
            dx = xp - xm
            dy = load(here, g, z, 1) - load(here, g, z, -1)
            dz = following - prev
            along = dx + (0.6 / 0.48) * dy + (0.64 / 0.48) * dz
            square = (4.0 + dx * dx) + (dy * dy + dz * dz)
            shading = 0.35 / GAIN + jnp.abs(along) * lax.rsqrt(square)
            absorbed, t1, t2, bell = (e_ref[i, 32 * z + 8 * g : 32 * z + 8 * g + 8, :] for i in range(4))
            weight = through * absorbed
            through = through - weight
            ws = weight * shading
            a0 = a0 + ws
            a1 = a1 + ws * t1
            a2 = a2 + ws * t2
            a3 = a3 + ws * bell
            state[at] = (c, following, through, a0, a1, a2, a3)
    return [one[2:] for one in state]


def march_half(trio, e_ref, o_ref, block, half):
    sets = []
    for through, a0, a1, a2, a3 in march(trio, e_ref, (2 * half, 2 * half + 1)):
        sets.append(
            (
                code((0.5 * GAIN) * (a0 + a1), COLOR_TOP),
                code((0.5 * GAIN) * (a0 - a2), COLOR_TOP),
                code(GAIN * a3, COLOR_TOP),
                code(-jnp.log2(through), TAU_TOP),
            )
        )
    for i in range(4):
        both = jnp.concatenate([sets[0][i], sets[1][i]], 0)
        o_ref[block, i, 16 * half : 16 * half + 16, :] = both.astype(jnp.int32).astype(jnp.int16)


def widening(w_ref):
    away = lax.broadcasted_iota(jnp.int32, (256, 256), 1) - 2 * lax.broadcasted_iota(jnp.int32, (256, 256), 0)
    w_ref[...] = jnp.where(away == 0, 0.25, jnp.where(jnp.abs(away) == 1, 0.125, 0.0)).astype(BF16)


def brick_kernel(a_hbm, above_hbm, below_hbm, coarse_hbm, lay_ref, o_ref, *scratch):
    a_ref, k_ref, w_ref, p_first, p_rest, d0, d1, d2, c0, c1, c2, h0, h1, h2, v0, v1, v2, v7 = scratch[:18]
    (e00, e01, e10, e11, e20, e21, e7), sem = scratch[18:25], scratch[25]
    cs, hs, ring, ds = (c0, c1, c2), (h0, h1, h2), (v0, v1, v2), (d0, d1, d2)
    es = ((e00, e01), (e10, e11), (e20, e21))
    copies = [
        pltpu.make_async_copy(of, to, sem.at[i])
        for i, (of, to) in enumerate(
            (
                (coarse_hbm, k_ref.at[pl.ds(0, 272)]),
                (above_hbm.at[:, pl.ds(2048, 1024)], k_ref.at[pl.ds(272, 32)]),
                (below_hbm.at[:, pl.ds(2048, 1024)], k_ref.at[pl.ds(304, 32)]),
                (a_hbm, a_ref.at[pl.ds(0, 1024)]),
                (above_hbm.at[:, pl.ds(0, 2048)], a_ref.at[pl.ds(1024, 32)]),
                (below_hbm.at[:, pl.ds(0, 2048)], a_ref.at[pl.ds(1056, 32)]),
            )
        )
    ]
    for copy in copies:
        copy.start()
    widening(w_ref)
    onehot(lay_ref, p_first, 0, TILES - 1)
    onehot(lay_ref, p_first, 1, 0)
    for copy in copies[:3]:
        copy.wait()
    coarse_tile(TILES - 1, k_ref, w_ref, c2, h2)
    coarse_tile(0, k_ref, w_ref, c0, h0)
    for copy in copies[3:]:
        copy.wait()
    matmul_tile(a_ref, p_first, 0, d0)
    matmul_tile(a_ref, p_first, 1, d1)
    for t in range(1, 7):
        onehot(lay_ref, p_rest, t - 1, t)
    values_tile(d0, h2, v7, (e7, None))
    values_tile(d0, h2, v2, (None, e21))
    matmul_tile(a_ref, p_rest, 0, d2)
    coarse_tile(1, k_ref, w_ref, c1, h1)
    values_tile(d1, h0, v0, es[0])

    def trios(prev, cur):
        return ((prev, 0), (prev, 1), (cur, 0)), ((prev, 1), (cur, 0), (cur, 1))

    def three(i, _):
        for j in range(3):
            s = 3 * i + j

            @pl.when(i < 2)
            def _(j=j, s=s):
                before, after = (j + 2) % 3, (j + 1) % 3
                one, two = trios(ring[before], ring[j])
                block = 2 * s - 1 if j else jnp.where(i == 0, BLOCKS - 1, 2 * s - 1)
                values_tile(ds[before], hs[after], ring[after], es[after])
                coarse_tile(jnp.minimum(s + 2, 7), k_ref, w_ref, cs[before], hs[before])
                matmul_tile(a_ref, p_rest, jnp.minimum(s + 1, 5), ds[j])
                march_half(one, es[before][1], o_ref, block, 0)
                march_half(one, es[before][1], o_ref, block, 1)
                march_half(two, es[j][0], o_ref, 2 * s, 0)
                march_half(two, es[j][0], o_ref, 2 * s, 1)

        return 0

    lax.fori_loop(0, 2, three, 0)
    for s, prev, cur, e_one, e_two in ((6, v2, v0, e21, e00), (7, v0, v7, e01, e7)):
        one, two = trios(prev, cur)
        for half in range(2):
            march_half(one, e_one, o_ref, 2 * s - 1, half)
            march_half(two, e_two, o_ref, 2 * s, half)


VMEM = pl.BlockSpec(memory_space=pltpu.VMEM)
ANY = pl.BlockSpec(memory_space=pl.ANY)


def brick(a, above, below, coarse, lay):
    return pl.pallas_call(
        brick_kernel,
        out_shape=jax.ShapeDtypeStruct((BLOCKS, 4, 32, 128), jnp.int16),
        in_specs=[ANY] * 4 + [VMEM],
        out_specs=VMEM,
        scratch_shapes=[
            pltpu.VMEM((1088, 2048), BF16),
            pltpu.VMEM((336, 1024), BF16),
            pltpu.VMEM((256, 256), BF16),
            pltpu.VMEM((2, 2048, 256), BF16),
            pltpu.VMEM((6, 2048, 256), BF16),
            *[pltpu.VMEM((1088, 256), F32)] * 3,
            *[pltpu.VMEM((2, 25 * CPITCH, 128), F32)] * 3,
            *[pltpu.VMEM((2, 25 * PITCH, 128), F32)] * 3,
            *[pltpu.VMEM((2, 33 * PITCH, 128), F32)] * 4,
            *[pltpu.VMEM((4, 1024, 128), F32)] * 7,
            pltpu.SemaphoreType.DMA((6,)),
        ],
        compiler_params=pltpu.CompilerParams(vmem_limit_bytes=58 * 2**20),
        name="brick",
    )(a, above, below, coarse, lay)


def composite_kernel(order_ref, parts_ref, o_ref):
    flip = order_ref[0]

    def image(b, i):
        x = parts_ref[b, i].astype(jnp.int32).astype(F32)
        top = TAU_TOP if i == 3 else COLOR_TOP
        return jnp.where(x > -32768.0, jnp.exp2((x - top) * (1.0 / STEPS)), 0.0)

    tau = jnp.zeros((32, 128), F32)
    sums = [jnp.zeros((32, 128), F32) for _ in range(3)]
    for rank in range(BLOCKS):
        b = rank ^ flip
        passing = jnp.exp2(-tau)
        for i in range(3):
            sums[i] = sums[i] + passing * image(b, i)
        tau = tau + image(b, 3)
    for i in range(3):
        o_ref[i] = sums[i]
    o_ref[3] = 1.0 - jnp.exp2(-tau)


def composite(order, parts):
    return pl.pallas_call(
        composite_kernel,
        out_shape=jax.ShapeDtypeStruct((4, 32, 128), F32),
        in_specs=[pl.BlockSpec(memory_space=pltpu.SMEM), VMEM],
        out_specs=VMEM,
        name="composite",
    )(order, parts)


def edge(detail, coarse, row, crow):
    lines = detail[:, row, :]
    fine = jnp.concatenate([lines[0::2], lines[1::2]], 0)
    rough = jnp.pad(coarse[:, crow, :], ((0, 15), (0, 0)))
    return jnp.concatenate([fine, rough], 1)


def on_device(coarse, detail, layout, view_order):
    n = lax.axis_size("rows")
    above = lax.ppermute(edge(detail, coarse, 31, 15), "rows", [(i, (i + 1) % n) for i in range(n)])
    below = lax.ppermute(edge(detail, coarse, 0, 0), "rows", [((i + 1) % n, i) for i in range(n)])
    codes = brick(detail.reshape(1024, 2048), above, below, coarse.reshape(272, 1024), layout.reshape(8, 256))
    parts = lax.all_to_all(codes, "depth", 0, 0, tiled=True)
    return composite(view_order, parts)


def solution(mesh):
    in_specs = (P("depth", "rows", None), P("depth", "rows", None), P(), P())
    out_specs = P(None, "rows", "depth")
    return jax.shard_map(on_device, mesh=mesh, in_specs=in_specs, out_specs=out_specs, check_vma=False)
```

time: 60.8 us -> 58.4 us (0.961)
  Pallas kernels: 28.8 us -> 27.6 us
  other arithmetic: 0.75 us -> 0.03 us
    slice x4 -> x0, local copies, waits for them, and re-layouts: 1.28 us -> none  [the longest x1 0.63 us: on_device(): above[:, 2048:]]
    pallas_call x1, Pallas kernels: 26.8 us -> 25.6 us  [brick(): pl.pallas_call(brick_kernel, out_shape=jax.ShapeDtypeStruct((BLOCKS, 4, 3...]
    unnamed x2 -> x6, local copies, waits for them, and re-layouts: 0.03 us -> 0.77 us
    concatenate x1 -> x0, other arithmetic: 0.71 us -> none  [on_device(): halo = jnp.concatenate([above[:, :2048], below[:, :2048]], 0)]
where the time goes in v2:
time: 58.4 us; the launch traced here: 58 us
  Pallas kernels  27.6 us (47%)
  blocking collectives  19.3 us (33%)
  local copies, waits for them, and re-layouts  5.57 us (10%)
  starting transfers between devices  3.59 us (6%)
  waiting for transfers between devices  1.89 us (3%)
    pallas_call x1, Pallas kernels, brick(): pl.pallas_call(brick_kernel, out_shape=jax.ShapeDtypeStruct((BLOCKS, 4, 3...  25.6 us
    all_to_all x1, blocking collectives, on_device(): parts = lax.all_to_all(codes, 'depth', 0, 0, tiled=True)  19.3 us
    ppermute x1, starting transfers between devices, on_device(): lax.ppermute(edge(detail, coarse, 0, 0), 'rows', [((i + 1) % n, i) for i...  3.57 us
    pallas_call x1, Pallas kernels, composite(): pl.pallas_call(composite_kernel, out_shape=jax.ShapeDtypeStruct((4, 32, 1...  2 us
    slice x1, local copies, waits for them, and re-layouts, edge(): lines = detail[:, row, :]  1.97 us
    ppermute x1, waiting for transfers between devices, on_device(): lax.ppermute(edge(detail, coarse, 31, 15), 'rows', [(i, (i + 1) % n) for...  1.87 us
    reshape x1, local copies, waits for them, and re-layouts, on_device(): layout.reshape(8, 256)  1.3 us
  transfers between devices with their start and end apart: 2, of which 1 were waited for; matrix products, arithmetic and copies ran while one was open for 2% of the time, Pallas kernels for 0%

profile of v2, /device:TPU:0, one launch (start us, length us, event | category | flops | bytes accessed | tf_op | source)
XLA Modules:
  0.0 58.0 jit_solution(17204328057717306094)
XLA Ops:
  0.0 2.0 %fusion.4 = (bf16[32,1,2048]{2,1,0:T(2,128)(2,1)S(1)}, bf16[32,1,2048]{2,1,0:T(2,128)(2,1)S(1)}) fusion(bf16[32,32,2048]{2,1,0:T(8,128)(2,1)} %param.5), kind=kLoop, calls=%fused_computation.9 | loop fusion | bytes 524288 | tf_op jit(solution)/shard_map/slice | solution.py:310
  2.0 0.2 copy_bitcast_fusion
  2.1 0.1 slice.26
  2.2 0.1 slice.25
  2.3 1.2 %fusion.5 = (bf16[17,1,1024]{2,1,0:T(2,128)(2,1)S(1)}, bf16[17,1,1024]{2,1,0:T(2,128)(2,1)S(1)}) fusion(bf16[17,16,1024]{2,1,0:T(8,128)(2,1)} %param.4), kind=kLoop, calls=%fused_computation.10 | loop fusion | bytes 139264 | tf_op jit(solution)/shard_map/slice | solution.py:312
  3.5 0.0 collective-permute-start
  3.5 0.1 slice.30
  3.5 0.1 slice.29
  3.7 3.6 %collective-permute-start.1 = (bf16[32,3072]{1,0:T(8,128)(2,1)S(1)}, bf16[32,3072]{1,0:T(8,128)(2,1)S(1)}, u32[]{:S(2)}, u32[]{:S(2)}) collective-permute-start(bf16[32,3072]{1,0:T(8,128)(2,1)S(1)} %fusion.3), channel_id=1, source_target_pairs={{1,0},{2,1},{3,2},{4,3},{5,4},{6,5},{7,6},{0,7},{9,8},{10,9},{11,1... | collective-permute-start | bytes 589832 | tf_op jit(solution)/shard_map/ppermute | solution.py:319
  7.2 1.3 %reshape.11.lay_ref = s32[8,256]{1,0:T(8,128)} reshape(s32[2048]{0:T(1024)} %param.6) | data formatting | bytes 16384 | tf_op jit(solution)/shard_map/reshape | solution.py:320
  8.5 1.9 %collective-permute-done.above_hbm = bf16[32,3072]{1,0:T(8,128)(2,1)S(1)} collective-permute-done((bf16[32,3072]{1,0:T(8,128)(2,1)S(1)}, bf16[32,3072]{1,0:T(8,128)(2,1)S(1)}, u32[]{:S(2)}, u32[]{:S(2)}) %collective-permute-start) | collective-permute-done | bytes 196640 | tf_op jit(solution)/shard_map/ppermute | solution.py:318
  10.4 0.0 copy-start
  10.4 0.0 collective-permute-done.1.below_hbm
  10.4 0.0 copy-start.1
  10.4 0.6 %copy-done = bf16[32,3072]{1,0:T(8,128)(2,1)} copy-done((bf16[32,3072]{1,0:T(8,128)(2,1)}, bf16[32,3072]{1,0:T(8,128)(2,1)S(1)}, u32[]{:S(2)}) %copy-start) | copy-done | bytes 196632
  11.1 0.1 copy-done.1
  11.2 25.6 %brick.1 = s16[16,4,32,128]{3,2,1,0:T(8,128)(2,1)} custom-call(bf16[1024,2048]{1,0:T(8,128)(2,1)} %bitcast.12, bf16[32,3072]{1,0:T(8,128)(2,1)} %copy-done, bf16[32,3072]{1,0:T(8,128)(2,1)} %copy-done.1, bf16[272,1024]{1,0:T(8,128)(2,1)} %bitcast.13, s32[8,256]{1,0:T(8,128)} %reshape.11.lay_ref), custom_call_target="tpu_custom_call" | custom-call | tf_op jit(solution)/shard_map/brick/pallas_call | solution.py:255
  36.7 19.3 %all_to_all.5.parts_ref = s16[16,4,32,128]{3,2,1,0:T(8,128)(2,1)} all-to-all(s16[16,4,32,128]{3,2,1,0:T(8,128)(2,1)} %brick.1), channel_id=1, replica_groups=mesh['depth'=16,'rows'=8] {'depth'}, dimensions={0} | all-to-all | bytes 1048576 | tf_op jit(solution)/shard_map/all_to_all | solution.py:321
  56.0 2.0 %composite.1 = f32[4,32,128]{2,1,0:T(8,128)} custom-call(s32[16]{0:T(128)} %order_ref.1, s16[16,4,32,128]{3,2,1,0:T(8,128)(2,1)} %all_to_all.5.parts_ref), custom_call_target="tpu_custom_call" | custom-call | tf_op jit(solution)/shard_map/composite/pallas_call | solution.py:300
  (4 shorter events, 0.1 us)
Async XLA Ops:
  3.5 6.9 %collective-permute-start = (bf16[32,3072]{1,0:T(8,128)(2,1)S(1)}, bf16[32,3072]{1,0:T(8,128)(2,1)S(1)}, u32[]{:S(2)}, u32[]{:S(2)}) collective-permute-start(bf16[32,3072]{1,0:T(8,128)(2,1)S(1)} %fusion.2), channel_id=1, source_target_pairs={{0,1},{1,2},{2,3},{3,4},{4,5},{5,6},{6,7},{7,0},{8,9},{9,10},{10,1... | collective-permute-start | bytes 589832 | tf_op jit(solution)/shard_map/ppermute | solution.py:318
  3.7 6.8 %collective-permute-start.1 = (bf16[32,3072]{1,0:T(8,128)(2,1)S(1)}, bf16[32,3072]{1,0:T(8,128)(2,1)S(1)}, u32[]{:S(2)}, u32[]{:S(2)}) collective-permute-start(bf16[32,3072]{1,0:T(8,128)(2,1)S(1)} %fusion.3), channel_id=1, source_target_pairs={{1,0},{2,1},{3,2},{4,3},{5,4},{6,5},{7,6},{0,7},{9,8},{10,9},{11,1... | collective-permute-start | bytes 589832 | tf_op jit(solution)/shard_map/ppermute | solution.py:319
  10.4 0.7 %copy-start = (bf16[32,3072]{1,0:T(8,128)(2,1)}, bf16[32,3072]{1,0:T(8,128)(2,1)S(1)}, u32[]{:S(2)}) copy-start(bf16[32,3072]{1,0:T(8,128)(2,1)S(1)} %collective-permute-done.above_hbm) | copy-start | bytes 589828
  10.4 0.7 %copy-start.1 = (bf16[32,3072]{1,0:T(8,128)(2,1)}, bf16[32,3072]{1,0:T(8,128)(2,1)S(1)}, u32[]{:S(2)}) copy-start(bf16[32,3072]{1,0:T(8,128)(2,1)S(1)} %collective-permute-done.1.below_hbm) | copy-start | bytes 589828

commit v3 on v2

--- a/solution.py
+++ b/solution.py
@@ -178,36 +178,43 @@
     w_ref[...] = jnp.where(away == 0, 0.25, jnp.where(jnp.abs(away) == 1, 0.125, 0.0)).astype(BF16)
 
 
-def brick_kernel(a_hbm, above_hbm, below_hbm, coarse_hbm, lay_ref, o_ref, *scratch):
+def brick_kernel(a_hbm, above_hbm, below_hbm, coarse_hbm, lay_hbm, o_hbm, *scratch):
     a_ref, k_ref, w_ref, p_first, p_rest, d0, d1, d2, c0, c1, c2, h0, h1, h2, v0, v1, v2, v7 = scratch[:18]
-    (e00, e01, e10, e11, e20, e21, e7), sem = scratch[18:25], scratch[25]
+    (e00, e01, e10, e11, e20, e21, e7), lay_ref, o_ref, sem, o_sem = scratch[18:25], *scratch[25:]
     cs, hs, ring, ds = (c0, c1, c2), (h0, h1, h2), (v0, v1, v2), (d0, d1, d2)
     es = ((e00, e01), (e10, e11), (e20, e21))
     copies = [
         pltpu.make_async_copy(of, to, sem.at[i])
         for i, (of, to) in enumerate(
             (
+                (lay_hbm, lay_ref),
                 (coarse_hbm, k_ref.at[pl.ds(0, 272)]),
                 (above_hbm.at[:, pl.ds(2048, 1024)], k_ref.at[pl.ds(272, 32)]),
                 (below_hbm.at[:, pl.ds(2048, 1024)], k_ref.at[pl.ds(304, 32)]),
-                (a_hbm, a_ref.at[pl.ds(0, 1024)]),
                 (above_hbm.at[:, pl.ds(0, 2048)], a_ref.at[pl.ds(1024, 32)]),
                 (below_hbm.at[:, pl.ds(0, 2048)], a_ref.at[pl.ds(1056, 32)]),
+                (a_hbm.at[:, pl.ds(0, 1024)], a_ref.at[pl.ds(0, 1024), pl.ds(0, 1024)]),
+                (a_hbm.at[:, pl.ds(1024, 1024)], a_ref.at[pl.ds(0, 1024), pl.ds(1024, 1024)]),
             )
         )
     ]
     for copy in copies:
         copy.start()
     widening(w_ref)
+    copies[0].wait()
     onehot(lay_ref, p_first, 0, TILES - 1)
     onehot(lay_ref, p_first, 1, 0)
-    for copy in copies[:3]:
+    for copy in copies[1:4]:
         copy.wait()
     coarse_tile(TILES - 1, k_ref, w_ref, c2, h2)
     coarse_tile(0, k_ref, w_ref, c0, h0)
-    for copy in copies[3:]:
+    for copy in copies[4:7]:
         copy.wait()
-    matmul_tile(a_ref, p_first, 0, d0)
+    for r in (0, HALF):
+        d0[r : r + HALF, :] = jnp.dot(a_ref[r : r + HALF, :1024], p_first[0, :1024, :], preferred_element_type=F32)
+    copies[7].wait()
+    for r in (0, HALF):
+        d0[r : r + HALF, :] += jnp.dot(a_ref[r : r + HALF, 1024:], p_first[0, 1024:, :], preferred_element_type=F32)
     matmul_tile(a_ref, p_first, 1, d1)
     for t in range(1, 7):
         onehot(lay_ref, p_rest, t - 1, t)
@@ -216,6 +223,9 @@
     matmul_tile(a_ref, p_rest, 0, d2)
     coarse_tile(1, k_ref, w_ref, c1, h1)
     values_tile(d1, h0, v0, es[0])
+
+    def leave(block):
+        return pltpu.make_async_copy(o_ref.at[block], o_hbm.at[block], o_sem.at[block])
 
     def trios(prev, cur):
         return ((prev, 0), (prev, 1), (cur, 0)), ((prev, 1), (cur, 0), (cur, 1))
@@ -234,8 +244,10 @@
                 matmul_tile(a_ref, p_rest, jnp.minimum(s + 1, 5), ds[j])
                 march_half(one, es[before][1], o_ref, block, 0)
                 march_half(one, es[before][1], o_ref, block, 1)
+                leave(block).start()
                 march_half(two, es[j][0], o_ref, 2 * s, 0)
                 march_half(two, es[j][0], o_ref, 2 * s, 1)
+                leave(2 * s).start()
 
         return 0
 
@@ -244,7 +256,12 @@
         one, two = trios(prev, cur)
         for half in range(2):
             march_half(one, e_one, o_ref, 2 * s - 1, half)
+        leave(2 * s - 1).start()
+        for half in range(2):
             march_half(two, e_two, o_ref, 2 * s, half)
+        leave(2 * s).start()
+    for block in range(BLOCKS):
+        leave(block).wait()
 
 
 VMEM = pl.BlockSpec(memory_space=pltpu.VMEM)
@@ -255,8 +272,8 @@
     return pl.pallas_call(
         brick_kernel,
         out_shape=jax.ShapeDtypeStruct((BLOCKS, 4, 32, 128), jnp.int16),
-        in_specs=[ANY] * 4 + [VMEM],
-        out_specs=VMEM,
+        in_specs=[ANY] * 5,
+        out_specs=ANY,
         scratch_shapes=[
             pltpu.VMEM((1088, 2048), BF16),
             pltpu.VMEM((336, 1024), BF16),
@@ -268,9 +285,12 @@
             *[pltpu.VMEM((2, 25 * PITCH, 128), F32)] * 3,
             *[pltpu.VMEM((2, 33 * PITCH, 128), F32)] * 4,
             *[pltpu.VMEM((4, 1024, 128), F32)] * 7,
-            pltpu.SemaphoreType.DMA((6,)),
+            pltpu.VMEM((8, 256), jnp.int32),
+            pltpu.VMEM((BLOCKS, 4, 32, 128), jnp.int16),
+            pltpu.SemaphoreType.DMA((8,)),
+            pltpu.SemaphoreType.DMA((BLOCKS,)),
         ],
-        compiler_params=pltpu.CompilerParams(vmem_limit_bytes=58 * 2**20),
+        compiler_params=pltpu.CompilerParams(vmem_limit_bytes=63 * 2**20),
         name="brick",
     )(a, above, below, coarse, lay)
 

time: 58.4 us -> 57.2 us (0.979)
  Pallas kernels: 27.6 us -> 26.4 us
    pallas_call x1, Pallas kernels: 25.6 us -> 24.4 us  [brick(): pl.pallas_call(brick_kernel, out_shape=jax.ShapeDtypeStruct((BLOCKS, 4, 3...]
  transfers between devices with their start and end apart: 2 -> 2, of which waited for: 1 -> 1; matrix products, arithmetic and copies ran while one was open for 2% -> 3% of each run, Pallas kernels for 0% -> 0%
where the time goes in v3:
time: 57.2 us; the launch traced here: 56.9 us
  Pallas kernels  26.4 us (46%)
  blocking collectives  19.3 us (34%)
  local copies, waits for them, and re-layouts  5.57 us (10%)
  starting transfers between devices  3.59 us (6%)
  waiting for transfers between devices  1.89 us (3%)
    pallas_call x1, Pallas kernels, brick(): pl.pallas_call(brick_kernel, out_shape=jax.ShapeDtypeStruct((BLOCKS, 4, 3...  24.4 us
    all_to_all x1, blocking collectives, on_device(): parts = lax.all_to_all(codes, 'depth', 0, 0, tiled=True)  19.3 us
    ppermute x1, starting transfers between devices, on_device(): lax.ppermute(edge(detail, coarse, 0, 0), 'rows', [((i + 1) % n, i) for i...  3.57 us
    pallas_call x1, Pallas kernels, composite(): pl.pallas_call(composite_kernel, out_shape=jax.ShapeDtypeStruct((4, 32, 1...  2 us
    slice x1, local copies, waits for them, and re-layouts, edge(): lines = detail[:, row, :]  1.97 us
    ppermute x1, waiting for transfers between devices, on_device(): lax.ppermute(edge(detail, coarse, 31, 15), 'rows', [(i, (i + 1) % n) for...  1.87 us
    reshape x1, local copies, waits for them, and re-layouts, on_device(): layout.reshape(8, 256)  1.3 us
    slice x1, local copies, waits for them, and re-layouts, edge(): rough = jnp.pad(coarse[:, crow, :], ((0, 15), (0, 0)))  1.15 us
  transfers between devices with their start and end apart: 2, of which 1 were waited for; matrix products, arithmetic and copies ran while one was open for 3% of the time, Pallas kernels for 0%

profile of v3, /device:TPU:0, one launch (start us, length us, event | category | flops | bytes accessed | tf_op | source)
XLA Modules:
  0.0 56.9 jit_solution(1233022747723463117)
XLA Ops:
  0.0 2.0 %fusion.4 = (bf16[32,1,2048]{2,1,0:T(2,128)(2,1)S(1)}, bf16[32,1,2048]{2,1,0:T(2,128)(2,1)S(1)}) fusion(bf16[32,32,2048]{2,1,0:T(8,128)(2,1)} %param.5), kind=kLoop, calls=%fused_computation.9 | loop fusion | bytes 524288 | tf_op jit(solution)/shard_map/slice | solution.py:330
  2.0 0.2 copy_bitcast_fusion
  2.1 0.1 slice.26
  2.2 0.1 slice.25
  2.3 1.2 %fusion.5 = (bf16[17,1,1024]{2,1,0:T(2,128)(2,1)S(1)}, bf16[17,1,1024]{2,1,0:T(2,128)(2,1)S(1)}) fusion(bf16[17,16,1024]{2,1,0:T(8,128)(2,1)} %param.4), kind=kLoop, calls=%fused_computation.10 | loop fusion | bytes 139264 | tf_op jit(solution)/shard_map/slice | solution.py:332
  3.5 0.0 collective-permute-start
  3.5 0.1 slice.30
  3.5 0.1 slice.29
  3.7 3.6 %collective-permute-start.1 = (bf16[32,3072]{1,0:T(8,128)(2,1)S(1)}, bf16[32,3072]{1,0:T(8,128)(2,1)S(1)}, u32[]{:S(2)}, u32[]{:S(2)}) collective-permute-start(bf16[32,3072]{1,0:T(8,128)(2,1)S(1)} %fusion.3), channel_id=1, source_target_pairs={{1,0},{2,1},{3,2},{4,3},{5,4},{6,5},{7,6},{0,7},{9,8},{10,9},{11,1... | collective-permute-start | bytes 589832 | tf_op jit(solution)/shard_map/ppermute | solution.py:339
  7.2 1.3 %reshape.11.lay_hbm = s32[8,256]{1,0:T(8,128)} reshape(s32[2048]{0:T(1024)} %param.6) | data formatting | bytes 16384 | tf_op jit(solution)/shard_map/reshape | solution.py:340
  8.5 1.9 %collective-permute-done.above_hbm = bf16[32,3072]{1,0:T(8,128)(2,1)S(1)} collective-permute-done((bf16[32,3072]{1,0:T(8,128)(2,1)S(1)}, bf16[32,3072]{1,0:T(8,128)(2,1)S(1)}, u32[]{:S(2)}, u32[]{:S(2)}) %collective-permute-start) | collective-permute-done | bytes 196640 | tf_op jit(solution)/shard_map/ppermute | solution.py:338
  10.4 0.0 copy-start
  10.4 0.0 collective-permute-done.1.below_hbm
  10.4 0.0 copy-start.1
  10.4 0.6 %copy-done = bf16[32,3072]{1,0:T(8,128)(2,1)} copy-done((bf16[32,3072]{1,0:T(8,128)(2,1)}, bf16[32,3072]{1,0:T(8,128)(2,1)S(1)}, u32[]{:S(2)}) %copy-start) | copy-done | bytes 196632
  11.1 0.1 copy-done.1
  11.2 24.4 %brick.1 = s16[16,4,32,128]{3,2,1,0:T(8,128)(2,1)} custom-call(bf16[1024,2048]{1,0:T(8,128)(2,1)} %bitcast.12, bf16[32,3072]{1,0:T(8,128)(2,1)} %copy-done, bf16[32,3072]{1,0:T(8,128)(2,1)} %copy-done.1, bf16[272,1024]{1,0:T(8,128)(2,1)} %bitcast.13, s32[8,256]{1,0:T(8,128)} %reshape.11.lay_hbm), custom_call_target="tpu_custom_call" | custom-call | tf_op jit(solution)/shard_map/brick/pallas_call | solution.py:272
  35.6 19.3 %all_to_all.5.parts_ref = s16[16,4,32,128]{3,2,1,0:T(8,128)(2,1)} all-to-all(s16[16,4,32,128]{3,2,1,0:T(8,128)(2,1)} %brick.1), channel_id=1, replica_groups=mesh['depth'=16,'rows'=8] {'depth'}, dimensions={0} | all-to-all | bytes 1048576 | tf_op jit(solution)/shard_map/all_to_all | solution.py:341
  54.9 2.0 %composite.1 = f32[4,32,128]{2,1,0:T(8,128)} custom-call(s32[16]{0:T(128)} %order_ref.1, s16[16,4,32,128]{3,2,1,0:T(8,128)(2,1)} %all_to_all.5.parts_ref), custom_call_target="tpu_custom_call" | custom-call | tf_op jit(solution)/shard_map/composite/pallas_call | solution.py:320
  (4 shorter events, 0.1 us)
Async XLA Ops:
  3.5 6.9 %collective-permute-start = (bf16[32,3072]{1,0:T(8,128)(2,1)S(1)}, bf16[32,3072]{1,0:T(8,128)(2,1)S(1)}, u32[]{:S(2)}, u32[]{:S(2)}) collective-permute-start(bf16[32,3072]{1,0:T(8,128)(2,1)S(1)} %fusion.2), channel_id=1, source_target_pairs={{0,1},{1,2},{2,3},{3,4},{4,5},{5,6},{6,7},{7,0},{8,9},{9,10},{10,1... | collective-permute-start | bytes 589832 | tf_op jit(solution)/shard_map/ppermute | solution.py:338
  3.7 6.8 %collective-permute-start.1 = (bf16[32,3072]{1,0:T(8,128)(2,1)S(1)}, bf16[32,3072]{1,0:T(8,128)(2,1)S(1)}, u32[]{:S(2)}, u32[]{:S(2)}) collective-permute-start(bf16[32,3072]{1,0:T(8,128)(2,1)S(1)} %fusion.3), channel_id=1, source_target_pairs={{1,0},{2,1},{3,2},{4,3},{5,4},{6,5},{7,6},{0,7},{9,8},{10,9},{11,1... | collective-permute-start | bytes 589832 | tf_op jit(solution)/shard_map/ppermute | solution.py:339
  10.4 0.7 %copy-start = (bf16[32,3072]{1,0:T(8,128)(2,1)}, bf16[32,3072]{1,0:T(8,128)(2,1)S(1)}, u32[]{:S(2)}) copy-start(bf16[32,3072]{1,0:T(8,128)(2,1)S(1)} %collective-permute-done.above_hbm) | copy-start | bytes 589828
  10.4 0.7 %copy-start.1 = (bf16[32,3072]{1,0:T(8,128)(2,1)}, bf16[32,3072]{1,0:T(8,128)(2,1)S(1)}, u32[]{:S(2)}) copy-start(bf16[32,3072]{1,0:T(8,128)(2,1)S(1)} %collective-permute-done.1.below_hbm) | copy-start | bytes 589828

commit v4 on v3

--- a/solution.py
+++ b/solution.py
@@ -208,6 +208,8 @@
         copy.wait()
     coarse_tile(TILES - 1, k_ref, w_ref, c2, h2)
     coarse_tile(0, k_ref, w_ref, c0, h0)
+    for t in range(1, 7):
+        onehot(lay_ref, p_rest, t - 1, t)
     for copy in copies[4:7]:
         copy.wait()
     for r in (0, HALF):
@@ -216,8 +218,6 @@
     for r in (0, HALF):
         d0[r : r + HALF, :] += jnp.dot(a_ref[r : r + HALF, 1024:], p_first[0, 1024:, :], preferred_element_type=F32)
     matmul_tile(a_ref, p_first, 1, d1)
-    for t in range(1, 7):
-        onehot(lay_ref, p_rest, t - 1, t)
     values_tile(d0, h2, v7, (e7, None))
     values_tile(d0, h2, v2, (None, e21))
     matmul_tile(a_ref, p_rest, 0, d2)

time: 57.2 us -> 56.8 us (level)
  no operation moved by 1% of the time
where the time goes in v4:
time: 56.8 us; the launch traced here: 56.4 us
  Pallas kernels  26 us (46%)
  blocking collectives  19.3 us (34%)
  local copies, waits for them, and re-layouts  5.57 us (10%)
  starting transfers between devices  3.59 us (6%)
  waiting for transfers between devices  1.89 us (3%)
    pallas_call x1, Pallas kernels, brick(): pl.pallas_call(brick_kernel, out_shape=jax.ShapeDtypeStruct((BLOCKS, 4, 3...  24 us
    all_to_all x1, blocking collectives, on_device(): parts = lax.all_to_all(codes, 'depth', 0, 0, tiled=True)  19.3 us
    ppermute x1, starting transfers between devices, on_device(): lax.ppermute(edge(detail, coarse, 0, 0), 'rows', [((i + 1) % n, i) for i...  3.57 us
    pallas_call x1, Pallas kernels, composite(): pl.pallas_call(composite_kernel, out_shape=jax.ShapeDtypeStruct((4, 32, 1...  2 us
    slice x1, local copies, waits for them, and re-layouts, edge(): lines = detail[:, row, :]  1.97 us
    ppermute x1, waiting for transfers between devices, on_device(): lax.ppermute(edge(detail, coarse, 31, 15), 'rows', [(i, (i + 1) % n) for...  1.87 us
    reshape x1, local copies, waits for them, and re-layouts, on_device(): layout.reshape(8, 256)  1.3 us
    slice x1, local copies, waits for them, and re-layouts, edge(): rough = jnp.pad(coarse[:, crow, :], ((0, 15), (0, 0)))  1.15 us
  transfers between devices with their start and end apart: 2, of which 1 were waited for; matrix products, arithmetic and copies ran while one was open for 3% of the time, Pallas kernels for 0%

profile of v4, /device:TPU:0, one launch (start us, length us, event | category | flops | bytes accessed | tf_op | source)
XLA Modules:
  0.0 56.4 jit_solution(7432534438088321165)
XLA Ops:
  0.0 2.0 %fusion.4 = (bf16[32,1,2048]{2,1,0:T(2,128)(2,1)S(1)}, bf16[32,1,2048]{2,1,0:T(2,128)(2,1)S(1)}) fusion(bf16[32,32,2048]{2,1,0:T(8,128)(2,1)} %param.5), kind=kLoop, calls=%fused_computation.9 | loop fusion | bytes 524288 | tf_op jit(solution)/shard_map/slice | solution.py:330
  2.0 0.2 copy_bitcast_fusion
  2.1 0.1 slice.26
  2.2 0.1 slice.25
  2.3 1.2 %fusion.5 = (bf16[17,1,1024]{2,1,0:T(2,128)(2,1)S(1)}, bf16[17,1,1024]{2,1,0:T(2,128)(2,1)S(1)}) fusion(bf16[17,16,1024]{2,1,0:T(8,128)(2,1)} %param.4), kind=kLoop, calls=%fused_computation.10 | loop fusion | bytes 139264 | tf_op jit(solution)/shard_map/slice | solution.py:332
  3.5 0.0 collective-permute-start
  3.5 0.1 slice.30
  3.5 0.1 slice.29
  3.7 3.6 %collective-permute-start.1 = (bf16[32,3072]{1,0:T(8,128)(2,1)S(1)}, bf16[32,3072]{1,0:T(8,128)(2,1)S(1)}, u32[]{:S(2)}, u32[]{:S(2)}) collective-permute-start(bf16[32,3072]{1,0:T(8,128)(2,1)S(1)} %fusion.3), channel_id=1, source_target_pairs={{1,0},{2,1},{3,2},{4,3},{5,4},{6,5},{7,6},{0,7},{9,8},{10,9},{11,1... | collective-permute-start | bytes 589832 | tf_op jit(solution)/shard_map/ppermute | solution.py:339
  7.2 1.3 %reshape.11.lay_hbm = s32[8,256]{1,0:T(8,128)} reshape(s32[2048]{0:T(1024)} %param.6) | data formatting | bytes 16384 | tf_op jit(solution)/shard_map/reshape | solution.py:340
  8.5 1.9 %collective-permute-done.above_hbm = bf16[32,3072]{1,0:T(8,128)(2,1)S(1)} collective-permute-done((bf16[32,3072]{1,0:T(8,128)(2,1)S(1)}, bf16[32,3072]{1,0:T(8,128)(2,1)S(1)}, u32[]{:S(2)}, u32[]{:S(2)}) %collective-permute-start) | collective-permute-done | bytes 196640 | tf_op jit(solution)/shard_map/ppermute | solution.py:338
  10.4 0.0 copy-start
  10.4 0.0 collective-permute-done.1.below_hbm
  10.4 0.0 copy-start.1
  10.4 0.6 %copy-done = bf16[32,3072]{1,0:T(8,128)(2,1)} copy-done((bf16[32,3072]{1,0:T(8,128)(2,1)}, bf16[32,3072]{1,0:T(8,128)(2,1)S(1)}, u32[]{:S(2)}) %copy-start) | copy-done | bytes 196632
  11.1 0.1 copy-done.1
  11.2 24.0 %brick.1 = s16[16,4,32,128]{3,2,1,0:T(8,128)(2,1)} custom-call(bf16[1024,2048]{1,0:T(8,128)(2,1)} %bitcast.12, bf16[32,3072]{1,0:T(8,128)(2,1)} %copy-done, bf16[32,3072]{1,0:T(8,128)(2,1)} %copy-done.1, bf16[272,1024]{1,0:T(8,128)(2,1)} %bitcast.13, s32[8,256]{1,0:T(8,128)} %reshape.11.lay_hbm), custom_call_target="tpu_custom_call" | custom-call | tf_op jit(solution)/shard_map/brick/pallas_call | solution.py:272
  35.2 19.3 %all_to_all.5.parts_ref = s16[16,4,32,128]{3,2,1,0:T(8,128)(2,1)} all-to-all(s16[16,4,32,128]{3,2,1,0:T(8,128)(2,1)} %brick.1), channel_id=1, replica_groups=mesh['depth'=16,'rows'=8] {'depth'}, dimensions={0} | all-to-all | bytes 1048576 | tf_op jit(solution)/shard_map/all_to_all | solution.py:341
  54.4 2.0 %composite.1 = f32[4,32,128]{2,1,0:T(8,128)} custom-call(s32[16]{0:T(128)} %order_ref.1, s16[16,4,32,128]{3,2,1,0:T(8,128)(2,1)} %all_to_all.5.parts_ref), custom_call_target="tpu_custom_call" | custom-call | tf_op jit(solution)/shard_map/composite/pallas_call | solution.py:320
  (4 shorter events, 0.1 us)
Async XLA Ops:
  3.5 6.9 %collective-permute-start = (bf16[32,3072]{1,0:T(8,128)(2,1)S(1)}, bf16[32,3072]{1,0:T(8,128)(2,1)S(1)}, u32[]{:S(2)}, u32[]{:S(2)}) collective-permute-start(bf16[32,3072]{1,0:T(8,128)(2,1)S(1)} %fusion.2), channel_id=1, source_target_pairs={{0,1},{1,2},{2,3},{3,4},{4,5},{5,6},{6,7},{7,0},{8,9},{9,10},{10,1... | collective-permute-start | bytes 589832 | tf_op jit(solution)/shard_map/ppermute | solution.py:338
  3.7 6.8 %collective-permute-start.1 = (bf16[32,3072]{1,0:T(8,128)(2,1)S(1)}, bf16[32,3072]{1,0:T(8,128)(2,1)S(1)}, u32[]{:S(2)}, u32[]{:S(2)}) collective-permute-start(bf16[32,3072]{1,0:T(8,128)(2,1)S(1)} %fusion.3), channel_id=1, source_target_pairs={{1,0},{2,1},{3,2},{4,3},{5,4},{6,5},{7,6},{0,7},{9,8},{10,9},{11,1... | collective-permute-start | bytes 589832 | tf_op jit(solution)/shard_map/ppermute | solution.py:339
  10.4 0.7 %copy-start = (bf16[32,3072]{1,0:T(8,128)(2,1)}, bf16[32,3072]{1,0:T(8,128)(2,1)S(1)}, u32[]{:S(2)}) copy-start(bf16[32,3072]{1,0:T(8,128)(2,1)S(1)} %collective-permute-done.above_hbm) | copy-start | bytes 589828
  10.4 0.7 %copy-start.1 = (bf16[32,3072]{1,0:T(8,128)(2,1)}, bf16[32,3072]{1,0:T(8,128)(2,1)S(1)}, u32[]{:S(2)}) copy-start(bf16[32,3072]{1,0:T(8,128)(2,1)S(1)} %collective-permute-done.1.below_hbm) | copy-start | bytes 589828
